TPU v7x, 512 devices: a whole 4x4x16 slice. The times are simulated.
512 devices in a mesh: chan: 128 (over x, z, core), row: 4 (over y).
Axes of the slice: x: 4, y: 4, z: 16, core: 2. Of those that a mesh axis runs over, the one named last changes fastest.
Arguments:
- amplitudes: bfloat16 [2048, 128, 640], P('row', 'chan'), may hold values from -6 to 6
- block_rows: int32 [128], P('chan'), may hold values from 256 to 2048, as said below
- recoupling: bfloat16 [128, 128], replicated, may hold values from -1 to 2
- interaction: bfloat16 [2048, 128, 2048], P(None, 'chan', 'row'), may hold values from -0.125 to 0.125
Outputs:
- residual: bfloat16 [2048, 128, 640], P('row', 'chan')
Inputs may be any that keep to these rules, and one draw needn't show every extreme that they name: `block_rows`: each entry is at least 256 and at most 2048; some channel has exactly 2048 live rows.
All inputs are finite; a program needn't handle non-finite values.
Results may differ from a plain program's by a relative error of at most 0.015.
Values may be sent and summed in bfloat16 or wider, within the bound.
A program may use at most 64 MiB of HBM per device.

v0:
```python
import jax
import jax.numpy as jnp
from jax import lax
from jax.sharding import PartitionSpec as P


def on_device(amplitudes, block_rows, recoupling, interaction):
    rows_here = amplitudes.shape[0]
    offset = lax.axis_index("row") * rows_here
    local_rows = offset + lax.iota(jnp.int32, rows_here)
    row_valid_mask = (local_rows[:, None] < block_rows[None, :])[:, :, None]
    zero = jnp.zeros((), jnp.bfloat16)
    masked = jnp.where(row_valid_mask, amplitudes, zero)
    spread = lax.all_to_all(masked, "chan", split_axis=0, concat_axis=1, tiled=True)
    mixed_rows = jnp.einsum(
        "kj,rjq->rkq", recoupling, spread, preferred_element_type=jnp.float32
    ).astype(jnp.bfloat16)
    crossing_row_set = lax.all_to_all(mixed_rows, "chan", split_axis=1, concat_axis=0, tiled=True)
    partials = jnp.einsum(
        "zmo,omu->zmu", interaction, crossing_row_set, preferred_element_type=jnp.float32
    )
    full_terms = partials.astype(jnp.bfloat16).astype(jnp.float32)
    reduced_total = lax.psum(full_terms.astype(jnp.bfloat16), "row").astype(jnp.float32)
    own_rows = lax.dynamic_slice_in_dim(reduced_total, offset, rows_here, 0)
    summed_rows = own_rows.astype(jnp.bfloat16)
    back_spread = lax.all_to_all(summed_rows, "chan", split_axis=0, concat_axis=1, tiled=True)
    unmixed = jnp.einsum(
        "jk,rjq->rkq", recoupling, back_spread, preferred_element_type=jnp.float32
    ).astype(jnp.bfloat16)
    back_rows = lax.all_to_all(unmixed, "chan", split_axis=1, concat_axis=0, tiled=True)
    return jnp.where(row_valid_mask, back_rows, zero)


def solution(mesh):
    return jax.shard_map(
        on_device,
        mesh=mesh,
        in_specs=(P("row", "chan", None), P("chan"), P(), P(None, "chan", "row")),
        out_specs=P("row", "chan", None),
        check_vma=False,
    )
```

profile of v0, /device:TPU:25, one launch (start us, length us, event | category | flops | bytes accessed | tf_op | source)
XLA Modules:
  0.0 328.6 jit_solution(16824926882113380921)
XLA Ops:
  7.4 1.2 broadcast_select_fusion.1
  8.6 0.5 broadcast.39
  9.1 1.1 reduce.2
  10.3 0.4 reshape.57
  10.7 57.8 %all_to_all.69 = bf16[128,2,1280]{2,1,0:T(2,128)(2,1)} all-to-all(bf16[128,2,1280]{2,1,0:T(2,128)(2,1)S(1)} %reshape.57), channel_id=1, replica_groups=mesh['chan'=128,'row'=4] {'chan'}, dimensions={0} | all-to-all | bytes 1310720 | tf_op jit(solution)/shard_map/all_to_all | solution.py:14
  68.4 4.1 %reshape.58 = bf16[512,1,640]{2,1,0:T(2,128)(2,1)S(1)} reshape(bf16[128,2,1280]{2,1,0:T(2,128)(2,1)} %all_to_all.69) | data formatting | bytes 1310720
  72.5 4.8 %reduce = bf16[512,640]{1,0:T(8,128)(2,1)} reduce(bf16[512,1,640]{2,1,0:T(2,128)(2,1)S(1)} %reshape.58, bf16[]{:T(256)} %constant.15), dimensions={1}, to_apply=%all_to_all.50.reduce_sub_computation | reduce | bytes 1310722 | tf_op jit(solution)/shard_map/all_to_all | solution.py:14
  77.3 1.6 all_to_all.51
  78.9 0.8 copy.12
  80.1 0.8 copy.13
  80.8 45.8 %all_to_all.70 = bf16[4,128,640]{2,0,1:T(4,128)(2,1)S(1)} all-to-all(bf16[4,128,640]{2,0,1:T(4,128)(2,1)S(1)} %copy.13), channel_id=1, replica_groups=mesh['chan'=128,'row'=4] {'chan'}, dimensions={1} | all-to-all | bytes 1310720 | tf_op jit(solution)/shard_map/all_to_all | solution.py:18
  126.8 3.1 fusion
  129.9 73.3 %all-reduce.2.cloned.1.call-done = bf16[2048,1,640]{0,2,1:T(8,128)(2,1)} async-done(((bf16[2048,1,640]{0,2,1:T(8,128)(2,1)}), bf16[2048,1,640]{0,2,1:T(8,128)(2,1)}) %all-reduce.2.cloned.1.call-update) | async-done | bytes 2621456 | tf_op jit(solution)/shard_map/psum | solution.py:23
  203.2 1.1 convert_convert_fusion
  204.4 1.1 reduce.3
  206.2 54.8 %all_to_all.71 = bf16[128,2,1280]{2,1,0:T(2,128)(2,1)} all-to-all(bf16[128,2,1280]{2,1,0:T(2,128)(2,1)S(1)} %reshape.59), channel_id=1, replica_groups=mesh['chan'=128,'row'=4] {'chan'}, dimensions={0} | all-to-all | bytes 1310720 | tf_op jit(solution)/shard_map/all_to_all | solution.py:26
  261.0 4.1 %reshape.60 = bf16[512,1,640]{2,1,0:T(2,128)(2,1)S(1)} reshape(bf16[128,2,1280]{2,1,0:T(2,128)(2,1)} %all_to_all.71) | data formatting | bytes 1310720
  265.1 4.8 %reduce.1 = bf16[512,640]{1,0:T(8,128)(2,1)} reduce(bf16[512,1,640]{2,1,0:T(2,128)(2,1)S(1)} %reshape.60, bf16[]{:T(256)} %constant.15), dimensions={1}, to_apply=%all_to_all.57.reduce_sub_computation | reduce | bytes 1310722 | tf_op jit(solution)/shard_map/all_to_all | solution.py:26
  269.9 1.6 all_to_all.58
  271.5 0.8 copy.15
  272.6 0.8 copy.16
  273.4 45.9 %all_to_all.72 = bf16[4,128,640]{2,0,1:T(4,128)(2,1)} all-to-all(bf16[4,128,640]{2,0,1:T(4,128)(2,1)S(1)} %copy.16), channel_id=1, replica_groups=mesh['chan'=128,'row'=4] {'chan'}, dimensions={1} | all-to-all | bytes 1310720 | tf_op jit(solution)/shard_map/all_to_all | solution.py:30
  319.3 1.5 all_to_all.64
  320.8 1.0 broadcast_select_fusion
  (12 shorter events, 1.5 us)
Async XLA Ops:
  6.5 120.3 %copy-start = (bf16[2048,1,512]{2,0,1:T(8,128)(2,1)S(1)}, bf16[2048,1,512]{2,0,1:T(8,128)(2,1)}, u32[]{:S(2)}) copy-start(bf16[2048,1,512]{2,0,1:T(8,128)(2,1)} %param.7) | copy-start | bytes 6291460
  6.5 196.7 %all-reduce.2.cloned.1.call-start = ((), (), s32[]{:S(2)}) async-start(), calls=%async_computation.4 | async-start | bytes 5242880 | tf_op jit(solution)/shard_map/psum | solution.py:23
  72.5 7.2 %copy-start.1 = (bf16[128,128]{1,0:T(8,128)(2,1)S(1)}, bf16[128,128]{1,0:T(8,128)(2,1)}, u32[]{:S(2)}) copy-start(bf16[128,128]{1,0:T(8,128)(2,1)} %param.6) | copy-start | bytes 98308
Sparse Core Ops, SparseCore 0:
  130.1 73.1 all-reduce.1
where the time goes:
time: 332 us; the launch traced here: 329 us
  blocking collectives  204 us (61%)
  waiting for transfers between devices  73.3 us (22%)
  local copies, waits for them, and re-layouts  17.7 us (5%)
  other arithmetic  15.2 us (5%)
  between operations  14.4 us (4%)
  matrix products  3.75 us (1%)
    psum x1, waiting for transfers between devices, on_device(): lax.psum(full_terms.astype(jnp.bfloat16), 'row').astype(jnp.float32)  73.3 us
    all_to_all x1, blocking collectives, on_device(): lax.all_to_all(masked, 'chan', split_axis=0, concat_axis=1, tiled=True)  57.8 us
    all_to_all x1, blocking collectives, on_device(): lax.all_to_all(summed_rows, 'chan', split_axis=0, concat_axis=1, tiled=True)  54.8 us
    all_to_all x1, blocking collectives, on_device(): lax.all_to_all(unmixed, 'chan', split_axis=1, concat_axis=0, tiled=True)  45.9 us
    all_to_all x1, blocking collectives, on_device(): lax.all_to_all(mixed_rows, 'chan', split_axis=1, concat_axis=0, tiled=True)  45.8 us
    unnamed x9, local copies, waits for them, and re-layouts  9.25 us
  transfers between devices with their start and end apart: 1, of which 1 were waited for; matrix products, arithmetic and copies ran while one was open for 0% of the time, Pallas kernels for 0%

commit v1 on v0

v1 whole, which is shorter than its diff:
```python
import jax
import jax.numpy as jnp
from jax import lax
from jax.experimental import pallas as pl
from jax.experimental.pallas import tpu as pltpu
from jax.sharding import PartitionSpec as P

MESH = pl.DeviceIdType.MESH
BF = jnp.bfloat16
F32 = jnp.float32

NX, NZ, NC, NY = 4, 16, 2, 4
NG = NX * NC
NCHAN = NG * NZ
ROWS = 512
SUB = ROWS // NCHAN
GB, ZB = ROWS // NG, ROWS // NZ
Q = 640
WIDTHS = (128,) * 5
STARTS = tuple(sum(WIDTHS[:i]) for i in range(len(WIDTHS)))
C = len(WIDTHS)

N_STEP = 10
BUFS = ("xs", "xr", "zs", "zr", "ms", "mr", "ps", "pr", "ss", "xr2", "zs2", "zr2", "ms2", "mr2", "ps2", "pr2")


def make_order():
    order = []
    for t in range(N_STEP + 2 * (C - 1)):
        for c in range(C):
            s = t - 2 * c
            if 0 <= s < N_STEP:
                order.append((s, c))
    return order


ORDER = make_order()


def chan_of_row(r):
    z, g = r // (NG * SUB), (r // SUB) % NG
    return ((g // NC) * NZ + z) * NC + g % NC


def dot(a, b):
    return lax.dot_general(a, b, (((1,), (0,)), ((), ())), preferred_element_type=F32)


def dot_nt(a, b):
    return lax.dot_general(a, b, (((1,), (1,)), ((), ())), preferred_element_type=F32)


def kernel(len_ref, amp_ref, rec_ref, int_ref, out_ref, *refs):
    bufs = []
    n = len(BUFS) + 2
    for c in range(C):
        mine = refs[c * n : (c + 1) * n]
        bufs.append(dict(zip(BUFS + ("ts", "tr"), mine)))
    inter, k1, k2, p1, p2, recv, send, load = refs[C * n :]

    chan, y = lax.axis_index("chan"), lax.axis_index("row")
    core, z, x = chan % NC, (chan // NC) % NZ, chan // (NC * NZ)
    g = x * NC + core

    def at_group(peer):
        return (((peer // NC) * NZ + z) * NC + peer % NC, y)

    def at_z(peer):
        return ((x * NZ + peer) * NC + core, y)

    def at_y(peer):
        return (chan, peer)

    barrier = pltpu.get_barrier_semaphore()

    def hail(count, me, where):
        def body(i, carry):
            pl.semaphore_signal(barrier, inc=1, device_id=where((me + i) % count), device_id_type=MESH)
            return carry

        lax.fori_loop(1, count, body, 0)

    hail(NG, g, at_group)
    hail(NZ, z, at_z)
    hail(NY, y, at_y)

    fetch = pltpu.make_async_copy(int_ref, inter, load)
    fetch.start()

    live = len_ref[0] - y * ROWS

    def masked(value):
        rows = lax.broadcasted_iota(jnp.int32, value.shape, 0)
        return jnp.where(rows < live, value.astype(F32), 0.0).astype(BF)

    def build():
        r = lax.broadcasted_iota(jnp.int32, (ROWS, NCHAN), 0)
        k = lax.broadcasted_iota(jnp.int32, (ROWS, NCHAN), 1)
        pick = (chan_of_row(r) == k).astype(F32).astype(BF)
        a = lax.broadcasted_iota(jnp.int32, (ROWS, ROWS), 0)
        b = lax.broadcasted_iota(jnp.int32, (ROWS, ROWS), 1)
        same = (a % SUB) == (b % SUB)
        rec = rec_ref[...]
        k1[...] = jnp.where(same, dot_nt(dot(pick, rec).astype(BF), pick), 0.0).astype(BF)
        k2[...] = jnp.where(same, dot_nt(dot_nt(pick, rec).astype(BF), pick), 0.0).astype(BF)
        there = ((a // SUB) % NG) * GB + (a // ZB) * SUB + a % SUB
        p1[...] = (there == b).astype(F32).astype(BF)
        back = ((b // SUB) % NG) * GB + (b // ZB) * SUB + b % SUB
        p2[...] = (back == a).astype(F32).astype(BF)

    def swap(stage, c, src, dst, count, me, rows, where):
        own = pl.ds(pl.multiple_of(me * rows, rows), rows)
        pltpu.make_async_copy(src.at[own], dst.at[own], recv.at[stage, c]).start()

        def body(i, carry):
            if count == NZ:
                odd = i % 2
                step = NZ // 2 + (1 - odd) * (i // 2) - odd * ((i + 1) // 2)
            else:
                step = i + 1
            peer = (me + step) % count
            pltpu.make_async_remote_copy(
                src_ref=src.at[pl.ds(pl.multiple_of(peer * rows, rows), rows)],
                dst_ref=dst.at[own],
                send_sem=send.at[stage, c],
                recv_sem=recv.at[stage, c],
                device_id=where(peer),
                device_id_type=MESH,
            ).start()
            return carry

        lax.fori_loop(0, count - 1, body, 0)

    def swap_group(stage, c, src, dst):
        swap(stage, c, bufs[c][src], bufs[c][dst], NG, g, GB, at_group)

    def swap_z(stage, c, src, dst):
        swap(stage, c, bufs[c][src], bufs[c][dst], NZ, z, ZB, at_z)

    def arrived(stage, c, dst):
        ref = bufs[c][dst]
        pltpu.make_async_copy(ref, ref, recv.at[stage, c]).wait()
        return ref

    def step(s, c):
        b, w = bufs[c], WIDTHS[c]
        cols = pl.ds(STARTS[c], w)
        if s == 0:
            b["xs"][...] = masked(amp_ref[:, cols])
            swap_group(0, c, "xs", "xr")
        elif s == 1:
            b["zs"][...] = dot(p1[...], arrived(0, c, "xr")[...]).astype(BF)
            swap_z(1, c, "zs", "zr")
        elif s == 2:
            b["ms"][...] = dot(k1[...], arrived(1, c, "zr")[...]).astype(BF)
            swap_z(2, c, "ms", "mr")
        elif s == 3:
            b["ps"][...] = dot(p2[...], arrived(2, c, "mr")[...]).astype(BF)
            swap_group(3, c, "ps", "pr")
        elif s == 4:
            cross = arrived(3, c, "pr")
            if c == 0:
                fetch.wait()

            def body(i, carry):
                peer = (y + 1 + i) % NY
                rows = pl.ds(pl.multiple_of(peer * ROWS, ROWS), ROWS)
                b["ts"][rows, :] = dot(inter[rows, :], cross[...]).astype(BF)

                @pl.when(i < NY - 1)
                def _():
                    pltpu.make_async_remote_copy(
                        src_ref=b["ts"].at[rows],
                        dst_ref=b["tr"].at[pl.ds(pl.multiple_of(i * ROWS, ROWS), ROWS)],
                        send_sem=send.at[4, c],
                        recv_sem=recv.at[4, c],
                        device_id=at_y(peer),
                        device_id_type=MESH,
                    ).start()

                return carry

            lax.fori_loop(0, NY, body, 0)
        elif s == 5:
            tr = arrived(4, c, "tr")
            total = b["ts"][pl.ds(pl.multiple_of(y * ROWS, ROWS), ROWS), :].astype(F32)
            for i in range(NY - 1):
                total = total + tr[pl.ds(i * ROWS, ROWS), :].astype(F32)
            b["ss"][...] = total.astype(BF)
            swap_group(5, c, "ss", "xr2")
        elif s == 6:
            b["zs2"][...] = dot(p1[...], arrived(5, c, "xr2")[...]).astype(BF)
            swap_z(6, c, "zs2", "zr2")
        elif s == 7:
            b["ms2"][...] = dot(k2[...], arrived(6, c, "zr2")[...]).astype(BF)
            swap_z(7, c, "ms2", "mr2")
        elif s == 8:
            b["ps2"][...] = dot(p2[...], arrived(7, c, "mr2")[...]).astype(BF)
            swap_group(8, c, "ps2", "pr2")
        else:
            out_ref[:, cols] = masked(arrived(8, c, "pr2")[...])

    pl.semaphore_wait(barrier, NG + NZ + NY - 3)
    for i, (s, c) in enumerate(ORDER):
        step(s, c)
        if i == 0:
            build()

    def sent(stage, c, ref, rows):
        part = ref.at[pl.ds(0, rows)]
        pltpu.make_async_copy(part, part, send.at[stage, c]).wait()

    for c in range(C):
        for stage in range(9):
            if stage == 4:
                sent(stage, c, bufs[c]["ts"], ROWS * (NY - 1))
            elif stage in (0, 3, 5, 8):
                sent(stage, c, bufs[c]["xs"], ROWS - GB)
            else:
                sent(stage, c, bufs[c]["xs"], ROWS - ZB)


def on_device(amplitudes, block_rows, recoupling, interaction):
    amp = amplitudes.reshape(ROWS, Q)
    inter = interaction.reshape(NY * ROWS, ROWS)
    scratch = []
    for w in WIDTHS:
        scratch += [pltpu.VMEM((ROWS, w), BF)] * len(BUFS)
        scratch += [pltpu.VMEM((NY * ROWS, w), BF), pltpu.VMEM(((NY - 1) * ROWS, w), BF)]
    scratch += [pltpu.VMEM((NY * ROWS, ROWS), BF)]
    scratch += [pltpu.VMEM((ROWS, ROWS), BF)] * 4
    scratch += [pltpu.SemaphoreType.DMA((9, C)), pltpu.SemaphoreType.DMA((9, C)), pltpu.SemaphoreType.DMA]
    out = pl.pallas_call(
        kernel,
        out_shape=jax.ShapeDtypeStruct((ROWS, Q), BF),
        in_specs=[
            pl.BlockSpec(memory_space=pltpu.SMEM),
            pl.BlockSpec(memory_space=pltpu.VMEM),
            pl.BlockSpec(memory_space=pltpu.VMEM),
            pl.BlockSpec(memory_space=pl.ANY),
        ],
        out_specs=pl.BlockSpec(memory_space=pltpu.VMEM),
        scratch_shapes=scratch,
        compiler_params=pltpu.CompilerParams(
            collective_id=0, has_side_effects=True, vmem_limit_bytes=48 * 1024 * 1024
        ),
        cost_estimate=pl.CostEstimate(flops=4 * 10**9, bytes_accessed=4 * 10**6, transcendentals=0),
    )(block_rows, amp, recoupling, inter)
    return out.reshape(ROWS, 1, Q)


def solution(mesh):
    return jax.shard_map(
        on_device,
        mesh=mesh,
        in_specs=(P("row", "chan", None), P("chan"), P(), P(None, "chan", "row")),
        out_specs=P("row", "chan", None),
        check_vma=False,
    )
```

time: 332 us -> 168 us (0.51); the launches traced: 329 us -> 168 us
  blocking collectives: 204 us -> 0 us
  Pallas kernels: 0 us -> 163 us
  waiting for transfers between devices: 73.3 us -> 0 us
  other arithmetic: 15.2 us -> 0 us
  between operations: 14.4 us -> 0.67 us
  local copies, waits for them, and re-layouts: 17.7 us -> 4.27 us
  matrix products: 3.75 us -> 0 us
    all_to_all x4 -> x0, blocking collectives: 204 us -> none  [the longest x1 57.8 us: on_device(): lax.all_to_all(masked, 'chan', split_axis=0, concat_axis=1, tiled=True)]
    pallas_call x0 -> x1, Pallas kernels: none -> 163 us  [on_device(): pl.pallas_call(kernel, out_shape=jax.ShapeDtypeStruct((ROWS, Q), BF), in_...]
    psum x1 -> x0, waiting for transfers between devices: 73.3 us -> none  [on_device(): lax.psum(full_terms.astype(jnp.bfloat16), 'row').astype(jnp.float32)]
    all_to_all x2 -> x0, other arithmetic: 9.63 us -> none  [the longest x1 4.82 us: on_device(): lax.all_to_all(masked, 'chan', split_axis=0, concat_axis=1, tiled=True)]
    all_to_all x5 -> x0, local copies, waits for them, and re-layouts: 6.23 us -> none  [the longest x2 2.37 us: on_device(): lax.all_to_all(summed_rows, 'chan', split_axis=0, concat_axis=1, tiled=True)]
    unnamed x9 -> x7, local copies, waits for them, and re-layouts: 9.25 us -> 4.27 us
    dot_general x3 -> x0, matrix products: 3.75 us -> none  [the longest x1 3.11 us: on_device(): jnp.einsum('zmo,omu->zmu', interaction, crossing_row_set, preferred_eleme...]
    select_n x3 -> x0, other arithmetic: 3.35 us -> none  [the longest x2 2.35 us: on_device(): masked = jnp.where(row_valid_mask, amplitudes, zero)]
  transfers between devices with their start and end apart: 1 -> 0, of which waited for: 1 -> 0; matrix products, arithmetic and copies ran while one was open for 0% -> 0% of each run, Pallas kernels for 0% -> 0%
where the time goes in v1:
time: 168 us
  Pallas kernels  163 us (97%)
  local copies, waits for them, and re-layouts  4.27 us (3%)
    pallas_call x1, Pallas kernels, on_device(): pl.pallas_call(kernel, out_shape=jax.ShapeDtypeStruct((ROWS, Q), BF), in_...  163 us
    unnamed x7, local copies, waits for them, and re-layouts  4.27 us

profile of v1, /device:TPU:25, one launch (start us, length us, event | category | flops | bytes accessed | tf_op | source)
XLA Modules:
  0.0 168.1 jit_solution(15973184652633446462)
XLA Ops:
  0.7 0.0 copy-start
  0.7 1.6 copy-done
  2.2 0.0 copy-start.1
  2.2 1.1 copy-done.1
  3.3 0.0 copy-start.2
  3.3 0.8 copy-done.2
  4.1 163.2 %shard_map.46 = bf16[512,640]{1,0:T(8,128)(2,1)S(1)} custom-call(s32[1]{0:T(128)S(6)} %copy.6.len_ref, bf16[512,640]{1,0:T(8,128)(2,1)S(1)} %bitcast.5, bf16[128,128]{1,0:T(8,128)(2,1)S(1)} %copy-done.2, bf16[2048,512]{1,0:T(8,128)(2,1)S(1)} %bitcast.4), custom_call_target="tpu_custom_call" | custom-call | flops 4000000000 | bytes 4000000 | tf_op jit(solution)/shard_map/pallas_call | solution.py:233
  167.3 0.8 copy.7
Async XLA Ops:
  0.7 1.6 copy-start
  2.2 1.1 copy-start.1
  3.3 0.8 copy-start.2

commit v2 on v1

v2 whole, which is shorter than its diff:
```python
import jax
import jax.numpy as jnp
from jax import lax
from jax.experimental import pallas as pl
from jax.experimental.pallas import tpu as pltpu
from jax.sharding import PartitionSpec as P

MESH = pl.DeviceIdType.MESH
BF = jnp.bfloat16
F32 = jnp.float32

NX, NZ, NC, NY = 4, 16, 2, 4
NG = NX * NC
NCHAN = NG * NZ
ROWS = 512
SUB = ROWS // NCHAN
GB, ZB = ROWS // NG, ROWS // NZ
Q = 640
WIDTHS = (128,) * 5
STARTS = tuple(sum(WIDTHS[:i]) for i in range(len(WIDTHS)))
C = len(WIDTHS)

ORDER = (
    (0, 0), (0, 1), (0, 2), (1, 0), (0, 3), (2, 0), (1, 1), (0, 4), (2, 1), (1, 2),
    (3, 0), (2, 2), (1, 3), (3, 1), (2, 3), (1, 4), (3, 2), (2, 4), (4, 0), (3, 3),
    (4, 1), (3, 4), (4, 2), (5, 0), (4, 3), (5, 1), (4, 4), (5, 2), (6, 0), (5, 3),
    (7, 0), (6, 1), (5, 4), (7, 1), (6, 2), (8, 0), (7, 2), (6, 3), (8, 1), (7, 3),
    (6, 4), (8, 2), (7, 4), (9, 0), (8, 3), (9, 1), (8, 4), (9, 2), (9, 3), (9, 4),
)

BUFS = ("z1", "z1r", "x1", "x1r", "x2", "x2r", "z2", "z2r", "z3", "z3r", "x3", "x3r", "x4", "x4r", "z4")
N_STAGE = 9


def chan_of_row(r):
    g, z = r // GB, (r // SUB) % NZ
    return ((g // NC) * NZ + z) * NC + g % NC


def dot(a, b):
    return lax.dot_general(a, b, (((1,), (0,)), ((), ())), preferred_element_type=F32)


def dot_nt(a, b):
    return lax.dot_general(a, b, (((1,), (1,)), ((), ())), preferred_element_type=F32)


def kernel(length, amp_any, rec_any, int_any, out_any, *refs):
    bufs = []
    n = len(BUFS) + 2
    for c in range(C):
        bufs.append(dict(zip(BUFS + ("ts", "tr"), refs[c * n : (c + 1) * n])))
    amp, inter, rec, k1, k2, p1, p2, recv, send, load = refs[C * n :]

    loads = []
    for c in range(C):
        cols = pl.ds(STARTS[c], WIDTHS[c])
        loads.append(pltpu.make_async_copy(amp_any.at[:, cols], amp.at[:, cols], load.at[c]))
    loads.append(pltpu.make_async_copy(rec_any, rec, load.at[C]))
    loads.append(pltpu.make_async_copy(int_any, inter, load.at[C + 1]))
    for copy in loads:
        copy.start()

    chan, y = lax.axis_index("chan"), lax.axis_index("row")
    core, z, x = chan % NC, (chan // NC) % NZ, chan // (NC * NZ)
    g = x * NC + core

    def at_group(peer):
        return (((peer // NC) * NZ + z) * NC + peer % NC, y)

    def at_z(peer):
        return ((x * NZ + peer) * NC + core, y)

    def at_y(peer):
        return (chan, peer)

    barrier = pltpu.get_barrier_semaphore()

    def hail(count, me, where):
        def body(i, carry):
            pl.semaphore_signal(barrier, inc=1, device_id=where((me + i) % count), device_id_type=MESH)
            return carry

        lax.fori_loop(1, count, body, 0)

    hail(NZ, z, at_z)
    hail(NG, g, at_group)
    hail(NY, y, at_y)

    def mask_in(c):
        loads[c].wait()
        value = amp[:, pl.ds(STARTS[c], WIDTHS[c])]
        rows = lax.broadcasted_iota(jnp.int32, value.shape, 0)
        live = rows < length[0] - y * ROWS
        bufs[c]["z1"][...] = jnp.where(live, value.astype(F32), 0.0).astype(BF)

    def build():
        r = lax.broadcasted_iota(jnp.int32, (ROWS, NCHAN), 0)
        k = lax.broadcasted_iota(jnp.int32, (ROWS, NCHAN), 1)
        pick = (chan_of_row(r) == k).astype(F32).astype(BF)
        a = lax.broadcasted_iota(jnp.int32, (ROWS, ROWS), 0)
        b = lax.broadcasted_iota(jnp.int32, (ROWS, ROWS), 1)
        same = (a % SUB) == (b % SUB)
        there = ((a // SUB) % NZ) * ZB + (a // GB) * SUB + a % SUB
        p1[...] = (there == b).astype(F32).astype(BF)
        back = ((b // SUB) % NZ) * ZB + (b // GB) * SUB + b % SUB
        p2[...] = (back == a).astype(F32).astype(BF)
        loads[C].wait()
        coef = rec[...]
        k1[...] = jnp.where(same, dot_nt(dot(pick, coef).astype(BF), pick), 0.0).astype(BF)
        k2[...] = jnp.where(same, dot_nt(dot_nt(pick, coef).astype(BF), pick), 0.0).astype(BF)

    def swap(stage, c, src, dst, count, me, rows, where):
        own = pl.ds(pl.multiple_of(me * rows, rows), rows)
        pltpu.make_async_copy(src.at[own], dst.at[own], recv.at[stage, c]).start()

        def body(i, carry):
            if count == NZ:
                odd = i % 2
                step = NZ // 2 + (1 - odd) * (i // 2) - odd * ((i + 1) // 2)
            else:
                step = i + 1
            peer = (me + step) % count
            pltpu.make_async_remote_copy(
                src_ref=src.at[pl.ds(pl.multiple_of(peer * rows, rows), rows)],
                dst_ref=dst.at[own],
                send_sem=send.at[stage, c],
                recv_sem=recv.at[stage, c],
                device_id=where(peer),
                device_id_type=MESH,
            ).start()
            return carry

        lax.fori_loop(0, count - 1, body, 0)

    def swap_group(stage, c, src, dst):
        swap(stage, c, bufs[c][src], bufs[c][dst], NG, g, GB, at_group)

    def out_cols(c):
        return out_any.at[:, pl.ds(STARTS[c], WIDTHS[c])]

    def swap_z(stage, c, src, dst):
        to = bufs[c][dst] if dst else out_cols(c)
        swap(stage, c, bufs[c][src], to, NZ, z, ZB, at_z)

    def arrived(stage, c, dst):
        ref = bufs[c][dst] if dst else out_cols(c)
        pltpu.make_async_copy(ref, ref, recv.at[stage, c]).wait()
        return ref

    def step(s, c):
        b = bufs[c]
        if s == 0:
            mask_in(c)
            swap_z(0, c, "z1", "z1r")
        elif s == 1:
            b["x1"][...] = dot(p1[...], arrived(0, c, "z1r")[...]).astype(BF)
            swap_group(1, c, "x1", "x1r")
        elif s == 2:
            b["x2"][...] = dot(k1[...], arrived(1, c, "x1r")[...]).astype(BF)
            swap_group(2, c, "x2", "x2r")
        elif s == 3:
            b["z2"][...] = dot(p2[...], arrived(2, c, "x2r")[...]).astype(BF)
            swap_z(3, c, "z2", "z2r")
        elif s == 4:
            cross = arrived(3, c, "z2r")
            if c == 0:
                loads[C + 1].wait()

            def body(i, carry):
                peer = (y + 1 + i) % NY
                rows = pl.ds(pl.multiple_of(peer * ROWS, ROWS), ROWS)
                b["ts"][rows, :] = dot(inter[rows, :], cross[...]).astype(BF)

                @pl.when(i < NY - 1)
                def _():
                    pltpu.make_async_remote_copy(
                        src_ref=b["ts"].at[rows],
                        dst_ref=b["tr"].at[pl.ds(pl.multiple_of(i * ROWS, ROWS), ROWS)],
                        send_sem=send.at[4, c],
                        recv_sem=recv.at[4, c],
                        device_id=at_y(peer),
                        device_id_type=MESH,
                    ).start()

                return carry

            lax.fori_loop(0, NY, body, 0)
        elif s == 5:
            tr = arrived(4, c, "tr")
            total = b["ts"][pl.ds(pl.multiple_of(y * ROWS, ROWS), ROWS), :].astype(F32)
            for i in range(NY - 1):
                total = total + tr[pl.ds(i * ROWS, ROWS), :].astype(F32)
            b["z3"][...] = total.astype(BF)
            swap_z(5, c, "z3", "z3r")
        elif s == 6:
            b["x3"][...] = dot(p1[...], arrived(5, c, "z3r")[...]).astype(BF)
            swap_group(6, c, "x3", "x3r")
        elif s == 7:
            b["x4"][...] = dot(k2[...], arrived(6, c, "x3r")[...]).astype(BF)
            swap_group(7, c, "x4", "x4r")
        elif s == 8:
            b["z4"][...] = dot(p2[...], arrived(7, c, "x4r")[...]).astype(BF)
            swap_z(8, c, "z4", None)
        else:
            arrived(8, c, None)

    pl.semaphore_wait(barrier, NG + NZ + NY - 3)
    for i, (s, c) in enumerate(ORDER):
        step(s, c)
        if i == 1:
            build()

    def sent(stage, c, ref, rows):
        part = ref.at[pl.ds(0, rows)]
        pltpu.make_async_copy(part, part, send.at[stage, c]).wait()

    for c in range(C):
        for stage in range(N_STAGE):
            if stage == 4:
                sent(stage, c, bufs[c]["ts"], ROWS * (NY - 1))
            elif stage in (0, 3, 5, 8):
                sent(stage, c, bufs[c]["z1"], ROWS - ZB)
            else:
                sent(stage, c, bufs[c]["z1"], ROWS - GB)


def on_device(amplitudes, block_rows, recoupling, interaction):
    amp = amplitudes.reshape(ROWS, Q)
    inter = interaction.reshape(NY * ROWS, ROWS)
    scratch = []
    for w in WIDTHS:
        scratch += [pltpu.VMEM((ROWS, w), BF)] * len(BUFS)
        scratch += [pltpu.VMEM((NY * ROWS, w), BF), pltpu.VMEM(((NY - 1) * ROWS, w), BF)]
    scratch += [pltpu.VMEM((ROWS, Q), BF), pltpu.VMEM((NY * ROWS, ROWS), BF), pltpu.VMEM((NCHAN, NCHAN), BF)]
    scratch += [pltpu.VMEM((ROWS, ROWS), BF)] * 4
    scratch += [pltpu.SemaphoreType.DMA((N_STAGE, C)), pltpu.SemaphoreType.DMA((N_STAGE, C))]
    scratch += [pltpu.SemaphoreType.DMA((C + 2,))]
    out = pl.pallas_call(
        kernel,
        out_shape=jax.ShapeDtypeStruct((ROWS, Q), BF),
        in_specs=[pl.BlockSpec(memory_space=pltpu.SMEM)] + [pl.BlockSpec(memory_space=pl.ANY)] * 3,
        out_specs=pl.BlockSpec(memory_space=pl.ANY),
        scratch_shapes=scratch,
        compiler_params=pltpu.CompilerParams(
            collective_id=0, has_side_effects=True, vmem_limit_bytes=60 * 1024 * 1024
        ),
        cost_estimate=pl.CostEstimate(flops=4 * 10**9, bytes_accessed=4 * 10**6, transcendentals=0),
    )(block_rows, amp, recoupling, inter)
    rows = lax.axis_index("row") * ROWS + lax.iota(jnp.int32, ROWS)
    live = (rows[:, None] < block_rows[None, :])[:, :, None]
    return jnp.where(live, out.reshape(ROWS, 1, Q), jnp.zeros((), BF))


def solution(mesh):
    return jax.shard_map(
        on_device,
        mesh=mesh,
        in_specs=(P("row", "chan", None), P("chan"), P(), P(None, "chan", "row")),
        out_specs=P("row", "chan", None),
        check_vma=False,
    )
```

time: 168 us -> 133 us (0.79)
  Pallas kernels: 163 us -> 129 us
  local copies, waits for them, and re-layouts: 4.27 us -> 0 us
  other arithmetic: 0 us -> 2.09 us
    pallas_call x1, Pallas kernels: 163 us -> 129 us  [on_device(): pl.pallas_call(kernel, out_shape=jax.ShapeDtypeStruct((ROWS, Q), BF), in_...]
    unnamed x7 -> x0, local copies, waits for them, and re-layouts: 4.27 us -> none
    select_n x0 -> x1, other arithmetic: none -> 2.09 us  [on_device(): return jnp.where(live, out.reshape(ROWS, 1, Q), jnp.zeros((), BF))]
where the time goes in v2:
time: 133 us; the launch traced here: 132 us
  Pallas kernels  129 us (97%)
  other arithmetic  2.09 us (2%)
    pallas_call x1, Pallas kernels, on_device(): pl.pallas_call(kernel, out_shape=jax.ShapeDtypeStruct((ROWS, Q), BF), in_...  129 us

profile of v2, /device:TPU:25, one launch (start us, length us, event | category | flops | bytes accessed | tf_op | source)
XLA Modules:
  0.0 132.0 jit_solution(16713018663180271047)
XLA Ops:
  0.7 129.3 %shard_map.46 = bf16[512,640]{1,0:T(8,128)(2,1)} custom-call(s32[1]{0:T(128)} %copy.5.length, bf16[512,640]{1,0:T(8,128)(2,1)} %bitcast.7, bf16[128,128]{1,0:T(8,128)(2,1)} %rec_any.1, bf16[2048,512]{1,0:T(8,128)(2,1)} %bitcast.6), custom_call_target="tpu_custom_call" | custom-call | flops 4000000000 | bytes 4000000 | tf_op jit(solution)/shard_map/pallas_call | solution.py:239
  129.9 2.1 %select_bitcast_fusion = bf16[512,1,640]{2,0,1:T(8,128)(2,1)} fusion(bf16[512,640]{1,0:T(8,128)(2,1)} %shard_map.46, pred[512]{0:T(512)(128)(4,1)S(1)} %add_compare_fusion), kind=kLoop, calls=%fused_computation | loop fusion | flops 327680 | bytes 1311232 | tf_op jit(solution)/shard_map/jit(_where)/select_n | solution.py:252
  (1 shorter events, 0.0 us)

commit v3 on v2

--- a/solution.py
+++ b/solution.py
@@ -58,8 +58,7 @@
         loads.append(pltpu.make_async_copy(amp_any.at[:, cols], amp.at[:, cols], load.at[c]))
     loads.append(pltpu.make_async_copy(rec_any, rec, load.at[C]))
     loads.append(pltpu.make_async_copy(int_any, inter, load.at[C + 1]))
-    for copy in loads:
-        copy.start()
+    loads[0].start()
 
     chan, y = lax.axis_index("chan"), lax.axis_index("row")
     core, z, x = chan % NC, (chan // NC) % NZ, chan // (NC * NZ)
@@ -77,15 +76,14 @@
     barrier = pltpu.get_barrier_semaphore()
 
     def hail(count, me, where):
-        def body(i, carry):
+        for i in range(1, count):
             pl.semaphore_signal(barrier, inc=1, device_id=where((me + i) % count), device_id_type=MESH)
-            return carry
-
-        lax.fori_loop(1, count, body, 0)
 
     hail(NZ, z, at_z)
     hail(NG, g, at_group)
     hail(NY, y, at_y)
+    for copy in loads[1:]:
+        copy.start()
 
     def mask_in(c):
         loads[c].wait()
@@ -115,12 +113,13 @@
         pltpu.make_async_copy(src.at[own], dst.at[own], recv.at[stage, c]).start()
 
         def body(i, carry):
-            if count == NZ:
+            if stage == 8 and c >= C - 2:
+                peer = i + (i >= me).astype(jnp.int32)
+            elif count == NZ:
                 odd = i % 2
-                step = NZ // 2 + (1 - odd) * (i // 2) - odd * ((i + 1) // 2)
+                peer = (me + NZ // 2 + (1 - odd) * (i // 2) - odd * ((i + 1) // 2)) % count
             else:
-                step = i + 1
-            peer = (me + step) % count
+                peer = (me + i + 1) % count
             pltpu.make_async_remote_copy(
                 src_ref=src.at[pl.ds(pl.multiple_of(peer * rows, rows), rows)],
                 dst_ref=dst.at[own],
@@ -151,7 +150,8 @@
     def step(s, c):
         b = bufs[c]
         if s == 0:
-            mask_in(c)
+            if c:
+                mask_in(c)
             swap_z(0, c, "z1", "z1r")
         elif s == 1:
             b["x1"][...] = dot(p1[...], arrived(0, c, "z1r")[...]).astype(BF)
@@ -205,24 +205,21 @@
         else:
             arrived(8, c, None)
 
+    def sent(stage, c):
+        rows = ROWS * (NY - 1) if stage == 4 else ROWS - (ZB if stage in (0, 3, 5, 8) else GB)
+        part = bufs[c]["ts"].at[pl.ds(0, rows)]
+        pltpu.make_async_copy(part, part, send.at[stage, c]).wait()
+
+    mask_in(0)
     pl.semaphore_wait(barrier, NG + NZ + NY - 3)
     for i, (s, c) in enumerate(ORDER):
         step(s, c)
+        if s >= 2:
+            sent(s - 2, c)
         if i == 1:
             build()
-
-    def sent(stage, c, ref, rows):
-        part = ref.at[pl.ds(0, rows)]
-        pltpu.make_async_copy(part, part, send.at[stage, c]).wait()
-
     for c in range(C):
-        for stage in range(N_STAGE):
-            if stage == 4:
-                sent(stage, c, bufs[c]["ts"], ROWS * (NY - 1))
-            elif stage in (0, 3, 5, 8):
-                sent(stage, c, bufs[c]["z1"], ROWS - ZB)
-            else:
-                sent(stage, c, bufs[c]["z1"], ROWS - GB)
+        sent(N_STAGE - 1, c)
 
 
 def on_device(amplitudes, block_rows, recoupling, interaction):
@@ -240,13 +237,13 @@
         kernel,
         out_shape=jax.ShapeDtypeStruct((ROWS, Q), BF),
         in_specs=[pl.BlockSpec(memory_space=pltpu.SMEM)] + [pl.BlockSpec(memory_space=pl.ANY)] * 3,
-        out_specs=pl.BlockSpec(memory_space=pl.ANY),
+        out_specs=pl.BlockSpec(memory_space=pltpu.VMEM),
         scratch_shapes=scratch,
         compiler_params=pltpu.CompilerParams(
-            collective_id=0, has_side_effects=True, vmem_limit_bytes=60 * 1024 * 1024
+            collective_id=0, has_side_effects=True, vmem_limit_bytes=44 * 1024 * 1024
         ),
         cost_estimate=pl.CostEstimate(flops=4 * 10**9, bytes_accessed=4 * 10**6, transcendentals=0),
-    )(block_rows, amp, recoupling, inter)
+    )(block_rows, *[pltpu.with_memory_space_constraint(v, pltpu.HBM) for v in (amp, recoupling, inter)])
     rows = lax.axis_index("row") * ROWS + lax.iota(jnp.int32, ROWS)
     live = (rows[:, None] < block_rows[None, :])[:, :, None]
     return jnp.where(live, out.reshape(ROWS, 1, Q), jnp.zeros((), BF))

time: 133 us -> 130 us (0.977)
    pallas_call x1, Pallas kernels: 129 us -> 128 us  [on_device(): pl.pallas_call(kernel, out_shape=jax.ShapeDtypeStruct((ROWS, Q), BF), in_...]
where the time goes in v3:
time: 130 us; the launch traced here: 129 us
  Pallas kernels  128 us (98%)
    pallas_call x1, Pallas kernels, on_device(): pl.pallas_call(kernel, out_shape=jax.ShapeDtypeStruct((ROWS, Q), BF), in_...  128 us

profile of v3, /device:TPU:25, one launch (start us, length us, event | category | flops | bytes accessed | tf_op | source)
XLA Modules:
  0.0 129.2 jit_solution(13669759878780564955)
XLA Ops:
  0.7 127.6 %shard_map.46 = bf16[512,640]{1,0:T(8,128)(2,1)S(1)} custom-call(s32[1]{0:T(128)} %copy.5.length, bf16[512,640]{1,0:T(8,128)(2,1)} %bitcast.7, bf16[128,128]{1,0:T(8,128)(2,1)} %rec_any.1, bf16[2048,512]{1,0:T(8,128)(2,1)} %bitcast.6), custom_call_target="tpu_custom_call" | custom-call | flops 4000000000 | bytes 4000000 | tf_op jit(solution)/shard_map/pallas_call | solution.py:236
  128.2 1.0 select_bitcast_fusion
  (1 shorter events, 0.0 us)

commit v4 on v3

--- a/solution.py
+++ b/solution.py
@@ -19,6 +19,8 @@
 WIDTHS = (128,) * 5
 STARTS = tuple(sum(WIDTHS[:i]) for i in range(len(WIDTHS)))
 C = len(WIDTHS)
+
+FIRST = 3
 
 ORDER = (
     (0, 0), (0, 1), (0, 2), (1, 0), (0, 3), (2, 0), (1, 1), (0, 4), (2, 1), (1, 2),
@@ -113,9 +115,7 @@
         pltpu.make_async_copy(src.at[own], dst.at[own], recv.at[stage, c]).start()
 
         def body(i, carry):
-            if stage == 8 and c >= C - 2:
-                peer = i + (i >= me).astype(jnp.int32)
-            elif count == NZ:
+            if count == NZ:
                 odd = i % 2
                 peer = (me + NZ // 2 + (1 - odd) * (i // 2) - odd * ((i + 1) // 2)) % count
             else:
@@ -141,6 +141,25 @@
     def swap_z(stage, c, src, dst):
         to = bufs[c][dst] if dst else out_cols(c)
         swap(stage, c, bufs[c][src], to, NZ, z, ZB, at_z)
+
+    own_z = pl.ds(pl.multiple_of(z * ZB, ZB), ZB)
+
+    def give_back(c, begin, end):
+        def body(peer, carry):
+            @pl.when(peer != z)
+            def _():
+                pltpu.make_async_remote_copy(
+                    src_ref=bufs[c]["z4"].at[pl.ds(pl.multiple_of(peer * ZB, ZB), ZB)],
+                    dst_ref=out_cols(c).at[own_z],
+                    send_sem=send.at[8, c],
+                    recv_sem=recv.at[8, c],
+                    device_id=at_z(peer),
+                    device_id_type=MESH,
+                ).start()
+
+            return carry
+
+        lax.fori_loop(begin, end, body, 0)
 
     def arrived(stage, c, dst):
         ref = bufs[c][dst] if dst else out_cols(c)
@@ -201,7 +220,14 @@
             swap_group(7, c, "x4", "x4r")
         elif s == 8:
             b["z4"][...] = dot(p2[...], arrived(7, c, "x4r")[...]).astype(BF)
-            swap_z(8, c, "z4", None)
+            if c < C - 2:
+                swap_z(8, c, "z4", None)
+            else:
+                pltpu.make_async_copy(b["z4"].at[own_z], out_cols(c).at[own_z], recv.at[8, c]).start()
+                give_back(c, 0, FIRST)
+            if c == C - 1:
+                give_back(C - 2, FIRST, NZ)
+                give_back(C - 1, FIRST, NZ)
         else:
             arrived(8, c, None)
 

time: 130 us -> 129 us (level)
  Pallas kernels: 128 us -> 125 us
    pallas_call x1, Pallas kernels: 128 us -> 125 us  [on_device(): pl.pallas_call(kernel, out_shape=jax.ShapeDtypeStruct((ROWS, Q), BF), in_...]
where the time goes in v4:
time: 129 us; the launch traced here: 127 us
  Pallas kernels  125 us (97%)
    pallas_call x1, Pallas kernels, on_device(): pl.pallas_call(kernel, out_shape=jax.ShapeDtypeStruct((ROWS, Q), BF), in_...  125 us

profile of v4, /device:TPU:25, one launch (start us, length us, event | category | flops | bytes accessed | tf_op | source)
XLA Modules:
  0.0 127.1 jit_solution(12481230162763026630)
XLA Ops:
  0.7 125.4 %shard_map.46 = bf16[512,640]{1,0:T(8,128)(2,1)S(1)} custom-call(s32[1]{0:T(128)} %copy.5.length, bf16[512,640]{1,0:T(8,128)(2,1)} %bitcast.7, bf16[128,128]{1,0:T(8,128)(2,1)} %rec_any.1, bf16[2048,512]{1,0:T(8,128)(2,1)} %bitcast.6), custom_call_target="tpu_custom_call" | custom-call | flops 4000000000 | bytes 4000000 | tf_op jit(solution)/shard_map/pallas_call | solution.py:262
  126.0 1.0 select_bitcast_fusion
  (1 shorter events, 0.0 us)

commit v5 on v4

--- a/solution.py
+++ b/solution.py
@@ -20,7 +20,7 @@
 STARTS = tuple(sum(WIDTHS[:i]) for i in range(len(WIDTHS)))
 C = len(WIDTHS)
 
-FIRST = 3
+FIRST, SECOND = 2, 5
 
 ORDER = (
     (0, 0), (0, 1), (0, 2), (1, 0), (0, 3), (2, 0), (1, 1), (0, 4), (2, 1), (1, 2),
@@ -226,8 +226,9 @@
                 pltpu.make_async_copy(b["z4"].at[own_z], out_cols(c).at[own_z], recv.at[8, c]).start()
                 give_back(c, 0, FIRST)
             if c == C - 1:
-                give_back(C - 2, FIRST, NZ)
-                give_back(C - 1, FIRST, NZ)
+                for begin, end in ((FIRST, SECOND), (SECOND, NZ)):
+                    give_back(C - 2, begin, end)
+                    give_back(C - 1, begin, end)
         else:
             arrived(8, c, None)
 

time: 129 us -> 129 us (level)
  the two profiles are of different devices: /device:TPU:25 before, /device:TPU:68 now
where the time goes in v5:
time: 129 us
  Pallas kernels  127 us (98%)
    pallas_call x1, Pallas kernels, on_device(): pl.pallas_call(kernel, out_shape=jax.ShapeDtypeStruct((ROWS, Q), BF), in_...  127 us

profile of v5, /device:TPU:68, one launch (start us, length us, event | category | flops | bytes accessed | tf_op | source)
XLA Modules:
  0.0 128.8 jit_solution(6241823263644530658)
XLA Ops:
  0.7 127.2 %shard_map.46 = bf16[512,640]{1,0:T(8,128)(2,1)S(1)} custom-call(s32[1]{0:T(128)} %copy.5.length, bf16[512,640]{1,0:T(8,128)(2,1)} %bitcast.7, bf16[128,128]{1,0:T(8,128)(2,1)} %rec_any.1, bf16[2048,512]{1,0:T(8,128)(2,1)} %bitcast.6), custom_call_target="tpu_custom_call" | custom-call | flops 4000000000 | bytes 4000000 | tf_op jit(solution)/shard_map/pallas_call | solution.py:263
  127.8 1.0 select_bitcast_fusion
  (1 shorter events, 0.0 us)

commit v6 on v5

--- a/solution.py
+++ b/solution.py
@@ -27,7 +27,7 @@
     (3, 0), (2, 2), (1, 3), (3, 1), (2, 3), (1, 4), (3, 2), (2, 4), (4, 0), (3, 3),
     (4, 1), (3, 4), (4, 2), (5, 0), (4, 3), (5, 1), (4, 4), (5, 2), (6, 0), (5, 3),
     (7, 0), (6, 1), (5, 4), (7, 1), (6, 2), (8, 0), (7, 2), (6, 3), (8, 1), (7, 3),
-    (6, 4), (8, 2), (7, 4), (9, 0), (8, 3), (9, 1), (8, 4), (9, 2), (9, 3), (9, 4),
+    (6, 4), (8, 2), (7, 4), (8, 3), (8, 4), (9, 0), (9, 1), (9, 2), (9, 3), (9, 4),
 )
 
 BUFS = ("z1", "z1r", "x1", "x1r", "x2", "x2r", "z2", "z2r", "z3", "z3r", "x3", "x3r", "x4", "x4r", "z4")

time: 129 us -> 129 us (level)
  the two profiles are of different devices: /device:TPU:68 before, /device:TPU:94 now
where the time goes in v6:
time: 129 us
  Pallas kernels  127 us (98%)
    pallas_call x1, Pallas kernels, on_device(): pl.pallas_call(kernel, out_shape=jax.ShapeDtypeStruct((ROWS, Q), BF), in_...  127 us

profile of v6, /device:TPU:94, one launch (start us, length us, event | category | flops | bytes accessed | tf_op | source)
XLA Modules:
  0.0 128.8 jit_solution(17615046249981809980)
XLA Ops:
  0.7 127.1 %shard_map.46 = bf16[512,640]{1,0:T(8,128)(2,1)S(1)} custom-call(s32[1]{0:T(128)} %copy.5.length, bf16[512,640]{1,0:T(8,128)(2,1)} %bitcast.7, bf16[128,128]{1,0:T(8,128)(2,1)} %rec_any.1, bf16[2048,512]{1,0:T(8,128)(2,1)} %bitcast.6), custom_call_target="tpu_custom_call" | custom-call | flops 4000000000 | bytes 4000000 | tf_op jit(solution)/shard_map/pallas_call | solution.py:263
  127.8 1.0 select_bitcast_fusion
  (1 shorter events, 0.0 us)
